TPU v7x, 256 devices: a whole 4x4x8 slice. The times are simulated.
256 devices in a mesh: dp: 8 (over y, z_hi), token: 32 (over x, z_lo, core).
Axes of the slice: x: 4, y: 4, z: 8 (z_hi: 2, z_lo: 4; z = z_hi * 4 + z_lo), core: 2. Of those that a mesh axis runs over, the one named last changes fastest.
Arguments:
- tokens: bfloat16 [2048, 32, 1024], P('dp', 'token'), may hold values from -6 to 6
- w_up: bfloat16 [32, 1024, 4096], P('token', None, 'dp'), may hold values from -0.1875 to 0.1875
- w_down: bfloat16 [32, 4096, 1024], P('token', 'dp'), may hold values from -0.09375 to 0.09375
- cotangent: bfloat16 [2048, 32, 1024], P('dp', 'token'), may hold values from -6 to 6
Outputs:
- output: bfloat16 [2048, 32, 1024], P('dp', 'token')
- grad_tokens: bfloat16 [2048, 32, 1024], P('dp', 'token')
- grad_up: float32 [32, 1024, 4096], P('token', None, 'dp')
- grad_down: float32 [32, 4096, 1024], P('token', 'dp')
All inputs are finite; a program needn't handle non-finite values.
Results may differ from a plain program's by a relative error of at most 0.014.
Values may be sent and summed in bfloat16 or wider, within the bound.
A program may use at most 128 MiB of HBM per device.

v0:
```python
import jax
import jax.numpy as jnp
from jax import lax
from jax.sharding import PartitionSpec as P

TOKENS = 32


EPSILON = 1e-05


def layer_norm(values):
    average = jnp.mean(values, axis=-1, keepdims=True)
    centred = values - average
    spread = jnp.mean(centred * centred, axis=-1, keepdims=True)
    scaling = lax.rsqrt(spread + EPSILON)
    return (centred * scaling, scaling)


def norm_back(normed, scaling, upstream):
    first = jnp.mean(upstream, axis=-1, keepdims=True)
    second = jnp.mean(upstream * normed, axis=-1, keepdims=True)
    return scaling * (upstream - first - normed * second)


def gelu_slope(hidden):
    return jax.grad(lambda inner: jnp.sum(jax.nn.gelu(inner)))(hidden)


def on_device(tokens, w_up, w_down, cotangent):
    local_rows, owned, feature_width = tokens.shape
    head_size = feature_width // TOKENS
    here_start = lax.axis_index("dp") * local_rows
    split_heads = tokens.reshape(local_rows, owned, TOKENS, head_size)
    arrived = lax.all_to_all(split_heads, "token", split_axis=2, concat_axis=1, tiled=True)
    mixed_in = arrived.transpose(0, 2, 1, 3).reshape(local_rows, owned, feature_width)
    summed = mixed_in.astype(jnp.float32) + tokens.astype(jnp.float32)
    normed_in, scale_in = layer_norm(summed)
    shared = normed_in.astype(jnp.bfloat16)
    all_shared = lax.all_gather(shared, "dp", axis=0, tiled=True)
    hidden = jnp.einsum("spd,pdf->spf", all_shared, w_up, preferred_element_type=jnp.float32)
    activ = jax.nn.gelu(hidden).astype(jnp.bfloat16)
    term_all = jnp.einsum("spf,pfd->spd", activ, w_down, preferred_element_type=jnp.float32)
    ffn_all = lax.psum(term_all.astype(jnp.bfloat16), "dp").astype(jnp.float32)
    normed_out, scale_out = layer_norm(ffn_all + all_shared.astype(jnp.float32))
    output = lax.dynamic_slice_in_dim(normed_out, here_start, local_rows, 0).astype(jnp.bfloat16)
    all_cotan = lax.all_gather(cotangent, "dp", axis=0, tiled=True)
    grad_out_all = norm_back(normed_out, scale_out, all_cotan.astype(jnp.float32))
    grad_ffn = grad_out_all.astype(jnp.bfloat16)
    grad_out = lax.dynamic_slice_in_dim(grad_out_all, here_start, local_rows, 0)
    grad_down = jnp.einsum("spf,spd->pfd", activ, grad_ffn, preferred_element_type=jnp.float32)
    grad_act = jnp.einsum("spd,pfd->spf", grad_ffn, w_down, preferred_element_type=jnp.float32)
    grad_hidden = (grad_act * gelu_slope(hidden)).astype(jnp.bfloat16)
    grad_up = jnp.einsum(
        "spd,spf->pdf", all_shared, grad_hidden, preferred_element_type=jnp.float32
    )
    grad_back = lax.psum_scatter(
        jnp.einsum("spf,pdf->spd", grad_hidden, w_up, preferred_element_type=jnp.float32).astype(
            jnp.bfloat16
        ),
        "dp",
        scatter_dimension=0,
        tiled=True,
    ).astype(jnp.float32)
    grad_shared = grad_back + grad_out
    grad_summed = norm_back(normed_in, scale_in, grad_shared)
    back_heads = grad_summed.astype(jnp.bfloat16).reshape(local_rows, owned, TOKENS, head_size)
    returned = lax.all_to_all(back_heads, "token", split_axis=2, concat_axis=1, tiled=True)
    back_mixed = returned.transpose(0, 2, 1, 3).reshape(local_rows, owned, feature_width)
    grad_tokens = (grad_summed + back_mixed.astype(jnp.float32)).astype(jnp.bfloat16)
    return (output, grad_tokens, grad_up, grad_down)


def solution(mesh):
    in_specs = (
        P("dp", "token", None),
        P("token", None, "dp"),
        P("token", "dp", None),
        P("dp", "token", None),
    )
    out_specs = (
        P("dp", "token", None),
        P("dp", "token", None),
        P("token", None, "dp"),
        P("token", "dp", None),
    )
    return jax.shard_map(
        on_device, mesh=mesh, in_specs=in_specs, out_specs=out_specs, check_vma=False
    )
```

profile of v0, /device:TPU:1, one launch (start us, length us, event | category | flops | bytes accessed | tf_op | source)
XLA Modules:
  0.0 788.7 jit_solution(14880838527174252144)
XLA Ops:
  7.2 1.4 copy.12
  8.6 26.6 %all_to_all.8 = bf16[256,1,32,32]{0,3,1,2:T(8,128)(2,1)S(1)} all-to-all(bf16[256,1,32,32]{0,3,1,2:T(8,128)(2,1)S(1)} %bitcast.106), channel_id=1, replica_groups=mesh['dp'=8,'token'=32] {'token'}, dimensions={2} | all-to-all | bytes 1048576 | tf_op jit(solution)/shard_map/all_to_all | solution.py:35
  35.4 1.2 fusion.57
  37.0 1.0 fusion.45
  38.0 104.9 %all-gather.3.cloned.1.call-done = bf16[2048,1,1024]{2,0,1:T(8,128)(2,1)} async-done(((bf16[256,1,1024]{2,0,1:T(8,128)(2,1)}), bf16[2048,1,1024]{2,0,1:T(8,128)(2,1)}) %all-gather.3.cloned.1.call-update) | async-done | bytes 4194320 | tf_op jit(solution)/shard_map/all_gather | solution.py:40
  142.9 4.8 fusion.22
  147.8 1.9 copy-done.7
  149.7 4.7 convert_bitcast_fusion.1
  155.3 346.5 %all-reduce.2.cloned.1.call-done = bf16[2048,1,1024]{2,0,1:T(8,128)(2,1)} async-done(((bf16[2048,1,1024]{2,0,1:T(8,128)(2,1)}), bf16[2048,1,1024]{2,0,1:T(8,128)(2,1)}) %all-reduce.2.cloned.1.call-update) | async-done | bytes 4194320 | tf_op jit(solution)/shard_map/psum | solution.py:44
  501.8 4.8 fusion.4
  506.5 1.1 copy-done.3
  507.7 1.8 multiply_reduce_fusion
  509.5 97.6 %all-gather.5.cloned.1.call-done = bf16[2048,1,1024]{2,0,1:T(8,128)(2,1)} async-done(((bf16[256,1,1024]{2,0,1:T(8,128)(2,1)}), bf16[2048,1,1024]{2,0,1:T(8,128)(2,1)}) %all-gather.5.cloned.1.call-update) | async-done | bytes 4194320 | tf_op jit(solution)/shard_map/all_gather | solution.py:47
  607.1 7.5 convert_reduce_fusion
  614.6 2.5 fusion.1
  617.1 1.7 copy-done.4
  618.8 1.0 copy-done.8
  619.8 4.7 fusion.26
  624.5 1.3 copy-done.11
  625.8 4.4 convert_bitcast_fusion
  630.3 6.5 fusion.33
  636.8 113.7 %reduce-scatter.2.cloned.1.call-done = bf16[256,1,1024]{2,0,1:T(8,128)(2,1)} async-done(((bf16[2048,1,1024]{2,0,1:T(8,128)(2,1)}), bf16[256,1,1024]{2,0,1:T(8,128)(2,1)}) %reduce-scatter.2.cloned.1.call-update) | async-done | bytes 524304 | tf_op jit(solution)/shard_map/reduce_scatter | solution.py:57
  750.5 1.8 fusion.48
  752.3 2.7 fusion.58
  755.0 1.0 copy.16
  756.0 6.4 all-to-all-start.1
  762.4 2.1 dynamic-slice_convert_fusion
  764.5 8.5 %fusion.36 = f32[1,512,1024]{2,1,0:T(8,128)} fusion(f32[2048,1,1024]{2,0,1:T(8,128)} %copy-done.2, f32[2048,512]{1,0:T(8,128)} %copy-done.7), kind=kOutput, calls=%fused_computation.41 | convolution fusion | flops 2159017984 | bytes 14680064 | tf_op jit(solution)/shard_map/spf,spd->pfd/dot_general | solution.py:51
  773.0 6.2 all-to-all-done.1
  779.2 0.8 copy-done.10
  780.0 1.2 copy.19
  781.3 0.9 add_convert_fusion
  (37 shorter events, 1.5 us)
Async XLA Ops:
  7.2 142.6 %copy-start = (bf16[1,512,1024]{2,1,0:T(8,128)(2,1)S(1)}, bf16[1,512,1024]{2,1,0:T(8,128)(2,1)}, u32[]{:S(2)}) copy-start(bf16[1,512,1024]{2,1,0:T(8,128)(2,1)} %param.6) | copy-start | bytes 3145732
  7.2 29.5 %copy-start.5 = (bf16[256,1,1024]{2,0,1:T(8,128)(2,1)S(1)}, bf16[256,1,1024]{2,0,1:T(8,128)(2,1)}, u32[]{:S(2)}) copy-start(bf16[256,1,1024]{2,0,1:T(8,128)(2,1)} %param.4) | copy-start | bytes 1572868
  7.2 135.8 %all-gather.3.cloned.1.call-start = ((), (), s32[]{:S(2)}) async-start(), calls=%async_computation.3 | async-start | bytes 4718592 | tf_op jit(solution)/shard_map/all_gather | solution.py:40
  38.0 463.8 %all-reduce.2.cloned.1.call-start = ((), (), s32[]{:S(2)}) async-start(), calls=%async_computation.4 | async-start | bytes 8388608 | tf_op jit(solution)/shard_map/psum | solution.py:44
  147.8 1.9 copy-start.7
  154.5 452.6 %all-gather.5.cloned.1.call-start = ((), (), s32[]{:S(2)}) async-start(), calls=%async_computation.5 | async-start | bytes 4718592 | tf_op jit(solution)/shard_map/all_gather | solution.py:47
  155.2 595.3 %reduce-scatter.2.cloned.1.call-start = ((), (), s32[]{:S(2)}) async-start(), calls=%async_computation.6 | async-start | bytes 4718592 | tf_op jit(solution)/shard_map/reduce_scatter | solution.py:57
  501.8 4.8 copy-start.1
  501.8 5.9 copy-start.3
  607.1 7.5 copy-start.6
  614.6 4.3 copy-start.4
  614.6 5.2 copy-start.8
  619.8 4.7 copy-start.2
  619.8 6.0 copy-start.12
  624.5 1.3 copy-start.11
  756.0 23.2 %all-to-all-start.1 = ((bf16[256,1,32,32]{0,3,1,2:T(8,128)(2,1)}), bf16[256,1,32,32]{0,3,1,2:T(8,128)(2,1)S(1)}, u32[]{:S(2)}, u32[]{:S(2)}) async-start(bf16[256,1,32,32]{0,3,1,2:T(8,128)(2,1)} %bitcast.25), calls=%async_computation.2 | async-start | bytes 1048576 | tf_op jit(solution)/shard_map/all_to_all | solution.py:68
  764.5 16.7 %copy-start.9 = (f32[256,1,1024]{2,0,1:T(8,128)S(1)}, f32[256,1,1024]{2,0,1:T(8,128)}, u32[]{:S(2)}) copy-start(f32[256,1,1024]{2,0,1:T(8,128)} %get-tuple-element.9) | copy-start | bytes 3145732
  779.2 0.8 copy-start.10
Sparse Core Ops, SparseCore 0:
  38.1 104.7 all-gather.2
  154.6 347.0 all-reduce.1
  504.4 102.6 all-gather.4
  630.4 120.0 reduce-scatter.1
where the time goes:
time: 789 us
  waiting for transfers between devices  670 us (85%)
  matrix products  33.7 us (4%)
  blocking collectives  26.6 us (3%)
  other arithmetic  24.5 us (3%)
  between operations  14 us (2%)
  local copies, waits for them, and re-layouts  13.8 us (2%)
    psum x1, waiting for transfers between devices, on_device(): ffn_all = lax.psum(term_all.astype(jnp.bfloat16), 'dp').astype(jnp.float32)  346 us
    reduce_scatter x1, waiting for transfers between devices, on_device(): lax.psum_scatter(jnp.einsum('spf,pdf->spd', grad_hidden, w_up, preferred_...  114 us
    all_gather x1, waiting for transfers between devices, on_device(): all_shared = lax.all_gather(shared, 'dp', axis=0, tiled=True)  105 us
    all_gather x1, waiting for transfers between devices, on_device(): all_cotan = lax.all_gather(cotangent, 'dp', axis=0, tiled=True)  97.6 us
    all_to_all x1, blocking collectives, on_device(): lax.all_to_all(split_heads, 'token', split_axis=2, concat_axis=1, tiled=T...  26.6 us
  transfers between devices with their start and end apart: 5, of which 5 were waited for; matrix products, arithmetic and copies ran while one was open for 3% of the time, Pallas kernels for 0%

commit v1 on v0

--- a/solution.py
+++ b/solution.py
@@ -30,7 +30,6 @@
 def on_device(tokens, w_up, w_down, cotangent):
     local_rows, owned, feature_width = tokens.shape
     head_size = feature_width // TOKENS
-    here_start = lax.axis_index("dp") * local_rows
     split_heads = tokens.reshape(local_rows, owned, TOKENS, head_size)
     arrived = lax.all_to_all(split_heads, "token", split_axis=2, concat_axis=1, tiled=True)
     mixed_in = arrived.transpose(0, 2, 1, 3).reshape(local_rows, owned, feature_width)
@@ -41,13 +40,13 @@
     hidden = jnp.einsum("spd,pdf->spf", all_shared, w_up, preferred_element_type=jnp.float32)
     activ = jax.nn.gelu(hidden).astype(jnp.bfloat16)
     term_all = jnp.einsum("spf,pfd->spd", activ, w_down, preferred_element_type=jnp.float32)
-    ffn_all = lax.psum(term_all.astype(jnp.bfloat16), "dp").astype(jnp.float32)
-    normed_out, scale_out = layer_norm(ffn_all + all_shared.astype(jnp.float32))
-    output = lax.dynamic_slice_in_dim(normed_out, here_start, local_rows, 0).astype(jnp.bfloat16)
-    all_cotan = lax.all_gather(cotangent, "dp", axis=0, tiled=True)
-    grad_out_all = norm_back(normed_out, scale_out, all_cotan.astype(jnp.float32))
-    grad_ffn = grad_out_all.astype(jnp.bfloat16)
-    grad_out = lax.dynamic_slice_in_dim(grad_out_all, here_start, local_rows, 0)
+    ffn = lax.psum_scatter(
+        term_all.astype(jnp.bfloat16), "dp", scatter_dimension=0, tiled=True
+    ).astype(jnp.float32)
+    normed_out, scale_out = layer_norm(ffn + shared.astype(jnp.float32))
+    output = normed_out.astype(jnp.bfloat16)
+    grad_out = norm_back(normed_out, scale_out, cotangent.astype(jnp.float32))
+    grad_ffn = lax.all_gather(grad_out.astype(jnp.bfloat16), "dp", axis=0, tiled=True)
     grad_down = jnp.einsum("spf,spd->pfd", activ, grad_ffn, preferred_element_type=jnp.float32)
     grad_act = jnp.einsum("spd,pfd->spf", grad_ffn, w_down, preferred_element_type=jnp.float32)
     grad_hidden = (grad_act * gelu_slope(hidden)).astype(jnp.bfloat16)

time: 789 us -> 558 us (0.71)
  waiting for transfers between devices: 670 us -> 456 us
  other arithmetic: 24.5 us -> 16.5 us
    psum x1 -> x0, waiting for transfers between devices: 346 us -> none  [on_device(): ffn_all = lax.psum(term_all.astype(jnp.bfloat16), 'dp').astype(jnp.float32)]
    reduce_scatter x0 -> x1, waiting for transfers between devices: none -> 121 us  [on_device(): lax.psum_scatter(term_all.astype(jnp.bfloat16), 'dp', scatter_dimension=0...]
  transfers between devices with their start and end apart: 5 -> 5, of which waited for: 5 -> 5; matrix products, arithmetic and copies ran while one was open for 3% -> 2% of each run, Pallas kernels for 0% -> 0%
where the time goes in v1:
time: 558 us
  waiting for transfers between devices  456 us (82%)
  matrix products  31.9 us (6%)
  blocking collectives  26.6 us (5%)
  other arithmetic  16.5 us (3%)
  between operations  13.9 us (2%)
  starting transfers between devices  6.72 us (1%)
  local copies, waits for them, and re-layouts  6.03 us (1%)
    reduce_scatter x1, waiting for transfers between devices, on_device(): lax.psum_scatter(jnp.einsum('spf,pdf->spd', grad_hidden, w_up, preferred_...  121 us
    reduce_scatter x1, waiting for transfers between devices, on_device(): lax.psum_scatter(term_all.astype(jnp.bfloat16), 'dp', scatter_dimension=0...  121 us
    all_gather x1, waiting for transfers between devices, on_device(): all_shared = lax.all_gather(shared, 'dp', axis=0, tiled=True)  105 us
    all_gather x1, waiting for transfers between devices, on_device(): lax.all_gather(grad_out.astype(jnp.bfloat16), 'dp', axis=0, tiled=True)  103 us
    all_to_all x1, blocking collectives, on_device(): lax.all_to_all(split_heads, 'token', split_axis=2, concat_axis=1, tiled=T...  26.6 us
  transfers between devices with their start and end apart: 5, of which 5 were waited for; matrix products, arithmetic and copies ran while one was open for 2% of the time, Pallas kernels for 0%

profile of v1, /device:TPU:1, one launch (start us, length us, event | category | flops | bytes accessed | tf_op | source)
XLA Modules:
  0.0 557.7 jit_solution(10683744087477086001)
XLA Ops:
  7.2 1.4 copy.12
  8.6 26.6 %all_to_all.8 = bf16[256,1,32,32]{0,3,1,2:T(8,128)(2,1)S(1)} all-to-all(bf16[256,1,32,32]{0,3,1,2:T(8,128)(2,1)S(1)} %bitcast.106), channel_id=1, replica_groups=mesh['dp'=8,'token'=32] {'token'}, dimensions={2} | all-to-all | bytes 1048576 | tf_op jit(solution)/shard_map/all_to_all | solution.py:34
  35.2 0.2 copy.15
  35.4 1.2 fusion.56
  36.7 0.3 multiply_reduce_fusion.2
  37.0 1.0 fusion.43
  38.0 0.0 reduce-scatter.3.cloned.1.call-start
  38.0 104.9 %all-gather.3.cloned.1.call-done = bf16[2048,1,1024]{2,0,1:T(8,128)(2,1)} async-done(((bf16[256,1,1024]{2,0,1:T(8,128)(2,1)}), bf16[2048,1,1024]{2,0,1:T(8,128)(2,1)}) %all-gather.3.cloned.1.call-update) | async-done | bytes 4194320 | tf_op jit(solution)/shard_map/all_gather | solution.py:39
  142.9 4.8 fusion.16
  147.8 1.9 copy-done.6
  149.7 4.8 convert_bitcast_fusion.1
  154.5 0.0 all-gather.5.cloned.1.call-start
  154.6 120.6 %reduce-scatter.3.cloned.1.call-done = bf16[256,1,1024]{2,0,1:T(8,128)(2,1)} async-done(((bf16[2048,1,1024]{2,0,1:T(8,128)(2,1)}), bf16[256,1,1024]{2,0,1:T(8,128)(2,1)}) %reduce-scatter.3.cloned.1.call-update) | async-done | bytes 524304 | tf_op jit(solution)/shard_map/reduce_scatter | solution.py:43
  275.2 1.3 fusion.41
  276.4 1.3 multiply_reduce_fusion.1
  277.8 1.7 convert_reduce_fusion
  279.5 2.9 fusion.58
  282.4 0.2 reduce-scatter.5.cloned.1.call-start
  282.6 103.4 %all-gather.5.cloned.1.call-done = bf16[2048,1,1024]{2,0,1:T(8,128)(2,1)} async-done(((bf16[256,1,1024]{2,0,1:T(8,128)(2,1)}), bf16[2048,1,1024]{2,0,1:T(8,128)(2,1)}) %all-gather.5.cloned.1.call-update) | async-done | bytes 4194320 | tf_op jit(solution)/shard_map/all_gather | solution.py:49
  386.0 7.4 %fusion.20 = bf16[2048,512]{1,0:T(8,128)(2,1)S(1)} fusion(f32[2048,512]{1,0:T(8,128)} %copy-done.6, bf16[2048,1,1024]{2,0,1:T(8,128)(2,1)} %all-gather.5.cloned.1.call-done, bf16[1,512,1024]{2,1,0:T(8,128)(2,1)S(1)} %copy-done), kind=kOutput, calls=%fused_computation.24 | convolution fusion | flops 2167406592 | bytes 11534336 | tf_op jit(solution)/shard_map/spd,pfd->spf/dot_general | solution.py:51
  393.4 1.3 copy-done.3
  394.7 4.3 convert_bitcast_fusion
  399.1 120.9 %reduce-scatter.5.cloned.1.call-done = bf16[256,1,1024]{2,0,1:T(8,128)(2,1)} async-done(((bf16[2048,1,1024]{2,0,1:T(8,128)(2,1)}), bf16[256,1,1024]{2,0,1:T(8,128)(2,1)}) %reduce-scatter.5.cloned.1.call-update) | async-done | bytes 524304 | tf_op jit(solution)/shard_map/reduce_scatter | solution.py:56
  520.0 1.8 fusion.47
  521.7 2.8 fusion.57
  524.6 1.0 copy.16
  525.6 6.4 %all-to-all-start.1 = ((bf16[256,1,32,32]{0,3,1,2:T(8,128)(2,1)}), bf16[256,1,32,32]{0,3,1,2:T(8,128)(2,1)S(1)}, u32[]{:S(2)}, u32[]{:S(2)}) async-start(bf16[256,1,32,32]{0,3,1,2:T(8,128)(2,1)} %bitcast.25), calls=%async_computation.3 | async-start | bytes 1048576 | tf_op jit(solution)/shard_map/all_to_all | solution.py:67
  532.0 6.7 %fusion.25 = f32[1,1024,512]{2,1,0:T(8,128)} fusion(bf16[2048,512]{1,0:T(8,128)(2,1)} %copy-done.3, bf16[2048,1,1024]{2,0,1:T(8,128)(2,1)} %all-gather.3.cloned.1.call-done), kind=kOutput, calls=%fused_computation.27 | convolution fusion | flops 2147483648 | bytes 8388608 | tf_op jit(solution)/shard_map/spd,spf->pdf/dot_general | solution.py:53
  538.7 3.9 fusion.28
  542.5 6.2 %all-to-all-done.1 = bf16[256,1,32,32]{0,3,1,2:T(8,128)(2,1)S(1)} async-done(((bf16[256,1,32,32]{0,3,1,2:T(8,128)(2,1)}), bf16[256,1,32,32]{0,3,1,2:T(8,128)(2,1)S(1)}, u32[]{:S(2)}, u32[]{:S(2)}) %all-to-all-start.1) | async-done | bytes 524320 | tf_op jit(solution)/shard_map/all_to_all | solution.py:67
  548.8 0.2 copy.19
  549.0 2.2 add_convert_fusion
  (26 shorter events, 0.2 us)
Async XLA Ops:
  7.2 142.6 %copy-start = (bf16[1,512,1024]{2,1,0:T(8,128)(2,1)S(1)}, bf16[1,512,1024]{2,1,0:T(8,128)(2,1)}, u32[]{:S(2)}) copy-start(bf16[1,512,1024]{2,1,0:T(8,128)(2,1)} %param.6) | copy-start | bytes 3145732
  7.2 29.5 %copy-start.2 = (bf16[256,1,1024]{2,0,1:T(8,128)(2,1)S(1)}, bf16[256,1,1024]{2,0,1:T(8,128)(2,1)}, u32[]{:S(2)}) copy-start(bf16[256,1,1024]{2,0,1:T(8,128)(2,1)} %param.4) | copy-start | bytes 1572868
  7.2 135.8 %all-gather.3.cloned.1.call-start = ((), (), s32[]{:S(2)}) async-start(), calls=%async_computation.4 | async-start | bytes 4718592 | tf_op jit(solution)/shard_map/all_gather | solution.py:39
  38.0 237.2 %reduce-scatter.3.cloned.1.call-start = ((), (), s32[]{:S(2)}) async-start(), calls=%async_computation.5 | async-start | bytes 4718592 | tf_op jit(solution)/shard_map/reduce_scatter | solution.py:43
  147.8 1.9 copy-start.6
  154.5 120.6 %copy-start.1 = (bf16[256,1,1024]{2,0,1:T(8,128)(2,1)S(1)}, bf16[256,1,1024]{2,0,1:T(8,128)(2,1)}, u32[]{:S(2)}) copy-start(bf16[256,1,1024]{2,0,1:T(8,128)(2,1)} %fusion.43) | copy-start | bytes 1572868
  154.5 231.5 %all-gather.5.cloned.1.call-start = ((), (), s32[]{:S(2)}) async-start(), calls=%async_computation.6 | async-start | bytes 4718592 | tf_op jit(solution)/shard_map/all_gather | solution.py:49
  282.4 237.6 %reduce-scatter.5.cloned.1.call-start = ((), (), s32[]{:S(2)}) async-start(), calls=%async_computation.7 | async-start | bytes 4718592 | tf_op jit(solution)/shard_map/reduce_scatter | solution.py:56
  386.0 8.7 %copy-start.5 = (bf16[1,1024,512]{2,1,0:T(8,128)(2,1)S(1)}, bf16[1,1024,512]{2,1,0:T(8,128)(2,1)}, u32[]{:S(2)}) copy-start(bf16[1,1024,512]{2,1,0:T(8,128)(2,1)} %param.5) | copy-start | bytes 3145732
  393.4 1.3 copy-start.3
  525.6 23.2 %all-to-all-start.1 = ((bf16[256,1,32,32]{0,3,1,2:T(8,128)(2,1)}), bf16[256,1,32,32]{0,3,1,2:T(8,128)(2,1)S(1)}, u32[]{:S(2)}, u32[]{:S(2)}) async-start(bf16[256,1,32,32]{0,3,1,2:T(8,128)(2,1)} %bitcast.25), calls=%async_computation.3 | async-start | bytes 1048576 | tf_op jit(solution)/shard_map/all_to_all | solution.py:67
  531.9 6.7 %copy-start.4 = (bf16[2048,1,1024]{2,0,1:T(8,128)(2,1)S(1)}, bf16[2048,1,1024]{2,0,1:T(8,128)(2,1)}, u32[]{:S(2)}) copy-start(bf16[2048,1,1024]{2,0,1:T(8,128)(2,1)} %all-gather.5.cloned.1.call-done) | copy-start | bytes 12582916
  532.0 6.7 %copy-start.7 = (f32[2048,512]{1,0:T(8,128)S(1)}, f32[2048,512]{1,0:T(8,128)}, u32[]{:S(2)}) copy-start(f32[2048,512]{1,0:T(8,128)} %copy-done.6) | copy-start | bytes 12582916
Sparse Core Ops, SparseCore 0:
  38.1 104.7 all-gather.2
  154.7 120.4 reduce-scatter.2
  282.5 103.4 all-gather.4
  399.2 120.6 reduce-scatter.4

commit v2 on v1

v2 whole, which is shorter than its diff:
```python
import functools

import jax
import jax.numpy as jnp
from jax import lax
from jax.experimental import pallas as pl
from jax.experimental.pallas import tpu as pltpu
from jax.sharding import PartitionSpec as P

MESH = pl.DeviceIdType.MESH
EPSILON = 1e-05
CHUNKS = 2
LANES = 128
GROUP = 4
WIDE = GROUP * LANES
MXU_ROWS = 256
F32 = jnp.float32
BF16 = jnp.bfloat16

MIX, MIX_BACK, UP, DOWN, GRAD_UP, GRAD_DOWN = 0, 2, 4, 5, 6, 7
GATHER, SCATTER, GATHER_BACK, SCATTER_BACK = 8, 14, 18, 24
COPIES = 28


def dot_nn(a, b):
    return jnp.dot(a, b, preferred_element_type=F32)


def dot_nt(a, b):
    return lax.dot_general(a, b, (((1,), (1,)), ((), ())), preferred_element_type=F32)


def layer_norm(values):
    centred = values - jnp.mean(values, axis=0, keepdims=True)
    scaling = lax.rsqrt(jnp.mean(centred * centred, axis=0, keepdims=True) + EPSILON)
    return centred * scaling, scaling


def norm_back(normed, scaling, upstream):
    first = jnp.mean(upstream, axis=0, keepdims=True)
    second = jnp.mean(upstream * normed, axis=0, keepdims=True)
    return scaling * (upstream - first - normed * second)


def gelu_and_slope(v):
    root = 0.7978845608028654
    square = v * v
    t = jnp.tanh(v * (root + (root * 0.044715) * square))
    half = 0.5 * (1.0 + t)
    inner = root + (3.0 * root * 0.044715) * square
    slope = half + (0.5 * v) * (1.0 - t * t) * inner
    return v * half, slope


def kernel(
    n_token, head,
    tok_ref, up_ref, down_ref, cot_ref,
    out_ref, gtok_ref, gup_ref, gdown_ref,
    tok_t, mixed, cot_t, up_far, down_far, up_t, down_t,
    shared, activ, slope, gffn, ghid,
    part_f, near_f, pass_f, far_f, part_b, near_b, pass_b, far_b,
    normed, scale_in, gout, gsum, gsum16, mixed_back,
    gup_out, gup_in, gdown_out, gdown_in,
    send, recv,
):
    dp = lax.axis_index("dp")
    me = lax.axis_index("token")
    y, zh = dp // 2, dp % 2
    dev_y = ((y + 1 - 2 * (y % 2)) * 2 + zh, me)
    dev_z = (y * 2 + 1 - zh, me)
    dev_w = ((3 - y) * 2 + zh, me)
    d_model, own = up_ref.shape

    def remote(src, dst, sem, device):
        return pltpu.make_async_remote_copy(
            src_ref=src, dst_ref=dst, send_sem=send.at[sem], recv_sem=recv.at[sem],
            device_id=device, device_id_type=MESH,
        )

    def piece(ref, c, p, n=1):
        return ref.at[:, pl.ds(c * WIDE + p * LANES, n * LANES)]

    def rows(i, n):
        return pl.ds(pl.multiple_of(i * n, n), n)

    barrier = pltpu.get_barrier_semaphore()

    @pl.loop(1, n_token)
    def _(i):
        pl.semaphore_signal(barrier, inc=1, device_id=(dp, (me + i) % n_token), device_id_type=MESH)

    for device in (dev_y, dev_z, dev_w):
        pl.semaphore_signal(barrier, inc=1, device_id=device, device_id_type=MESH)

    @pl.loop(0, d_model // LANES)
    def _(i):
        block = tok_ref[:, rows(i, LANES)].T
        for c in range(CHUNKS):
            tok_t[c, rows(i, LANES), :] = block[:, c * LANES:(c + 1) * LANES]

    pl.semaphore_wait(barrier, n_token + 2)

    w_up = remote(up_ref, up_far, UP, dev_w)
    w_down = remote(down_ref, down_far, DOWN, dev_w)

    def mix_start(src, dst, sem, c):
        @pl.loop(1, n_token)
        def _(i):
            to = (me + i) % n_token
            remote(
                src.at[c, rows(to, head), :], dst.at[c, rows(me, head), :], sem + c, (dp, to)
            ).start()

        dst[c, rows(me, head), :] = src[c, rows(me, head), :]

    def mix_wait(src, dst, sem, c):
        span = pl.ds(0, (n_token - 1) * head)
        whole = remote(src.at[c, span, :], dst.at[c, span, :], sem + c, dev_y)
        whole.wait_send()
        whole.wait_recv()

    def gather(ref, sem, c):
        return (
            remote(piece(ref, c, 0), piece(ref, c, 2), sem + c, dev_y),
            remote(piece(ref, c, 0), piece(ref, c, 1), sem + 2 + c, dev_z),
            remote(piece(ref, c, 1), piece(ref, c, 3), sem + 4 + c, dev_y),
        )

    def scatter(part, near, passed, far, sem, c):
        return (
            remote(piece(part, c, 2, 2), near.at[c], sem + c, dev_y),
            remote(passed.at[c], far.at[c], sem + 2 + c, dev_z),
        )

    gathers = [gather(shared, GATHER, c) for c in range(CHUNKS)]
    scatters = [scatter(part_f, near_f, pass_f, far_f, SCATTER, c) for c in range(CHUNKS)]
    gathers_b = [gather(gffn, GATHER_BACK, c) for c in range(CHUNKS)]
    scatters_b = [scatter(part_b, near_b, pass_b, far_b, SCATTER_BACK, c) for c in range(CHUNKS)]
    g_up = remote(gup_out, gup_in, GRAD_UP, dev_w)
    g_down = remote(gdown_out, gdown_in, GRAD_DOWN, dev_w)

    def transpose_up(src, half):
        @pl.loop(0, own // LANES)
        def _(i):
            up_t[pl.ds(pl.multiple_of(half * own + i * LANES, LANES), LANES), :] = src[:, rows(i, LANES)].T

    def transpose_down(src, half):
        @pl.loop(0, d_model // LANES)
        def _(i):
            down_t[rows(i, LANES), pl.ds(half * own, own)] = src[:, rows(i, LANES)].T

    def norm_in(c):
        summed = mixed[c].astype(F32) + tok_t[c].astype(F32)
        value, scaling = layer_norm(summed)
        normed[c] = value
        scale_in[c, 0:1, :] = scaling
        shared[:, c * WIDE:c * WIDE + LANES] = value.astype(BF16)

    def up(c):
        span = pl.ds(c * WIDE, WIDE)

        @pl.loop(0, 2 * own // MXU_ROWS)
        def _(i):
            r = rows(i, MXU_ROWS)
            hidden = dot_nn(up_t[r, :], shared[:, span])
            value, grade = gelu_and_slope(hidden)
            activ[r, span] = value.astype(BF16)
            slope[r, span] = grade.astype(BF16)

    def down(c, p):
        span = pl.ds(c * WIDE + p * LANES, 2 * LANES)

        @pl.loop(0, d_model // MXU_ROWS)
        def _(i):
            r = rows(i, MXU_ROWS)
            part_f[r, span] = dot_nn(down_t[r, :], activ[:, span]).astype(BF16)

    def add_near(part, near, passed, c):
        passed[c] = (
            part[:, c * WIDE + LANES:c * WIDE + 2 * LANES].astype(F32) + near[c, :, LANES:].astype(F32)
        ).astype(BF16)

    def total(part, near, far, c):
        return (
            part[:, c * WIDE:c * WIDE + LANES].astype(F32)
            + near[c, :, :LANES].astype(F32)
            + far[c].astype(F32)
        )

    def norm_out(c):
        ffn = total(part_f, near_f, far_f, c)
        value, scaling = layer_norm(ffn + shared[:, c * WIDE:c * WIDE + LANES].astype(F32))
        part_f[:, c * WIDE:c * WIDE + LANES] = value.astype(BF16)
        grad = norm_back(value, scaling, cot_t[c].astype(F32))
        gout[c] = grad
        gffn[:, c * WIDE:c * WIDE + LANES] = grad.astype(BF16)

    def write_out(c):
        @pl.loop(0, d_model // LANES)
        def _(i):
            out_ref[pl.ds(c * LANES, LANES), rows(i, LANES)] = part_f[rows(i, LANES), pl.ds(c * WIDE, LANES)].T

    def hidden_back(c):
        span = pl.ds(c * WIDE, WIDE)
        for half, src in enumerate((down_ref, down_far)):
            @pl.loop(0, own // MXU_ROWS)
            def _(i):
                r = pl.ds(pl.multiple_of(half * own + i * MXU_ROWS, MXU_ROWS), MXU_ROWS)
                grad = dot_nn(src[rows(i, MXU_ROWS), :], gffn[:, span])
                ghid[r, span] = (grad * slope[r, span].astype(F32)).astype(BF16)

    def shared_back(c, p):
        span = pl.ds(c * WIDE + p * LANES, 2 * LANES)

        @pl.loop(0, d_model // MXU_ROWS)
        def _(i):
            r = rows(i, MXU_ROWS)
            part_b[r, span] = (
                dot_nn(up_ref[r, :], ghid[pl.ds(0, own), span])
                + dot_nn(up_far[r, :], ghid[pl.ds(own, own), span])
            ).astype(BF16)

    def sum_back(c):
        grad = total(part_b, near_b, far_b, c) + gout[c]
        grad = norm_back(normed[c], scale_in[c, 0:1, :], grad)
        gsum[c] = grad
        gsum16[c] = grad.astype(BF16)

    def tokens_back(c):
        @pl.loop(0, d_model // LANES)
        def _(i):
            r = rows(i, LANES)
            value = (gsum[c, r, :] + mixed_back[c, r, :].astype(F32)).astype(BF16)
            gtok_ref[pl.ds(c * LANES, LANES), r] = value.T

    def grad_down(half, dst):
        @pl.loop(0, own // MXU_ROWS)
        def _(i):
            r = pl.ds(pl.multiple_of(half * own + i * MXU_ROWS, MXU_ROWS), MXU_ROWS)
            dst[rows(i, MXU_ROWS), :] = dot_nt(activ[r, :], gffn[...]).astype(dst.dtype)

    def grad_up(half, dst):
        @pl.loop(0, d_model // MXU_ROWS)
        def _(i):
            r = rows(i, MXU_ROWS)
            dst[r, :] = dot_nt(shared[r, :], ghid[pl.ds(half * own, own), :]).astype(dst.dtype)

    for c in range(CHUNKS):
        mix_start(tok_t, mixed, MIX, c)
    w_up.start()
    w_down.start()
    transpose_up(up_ref, 0)
    transpose_down(down_ref, 0)

    @pl.loop(0, d_model // LANES)
    def _(i):
        block = cot_ref[:, rows(i, LANES)].T
        for c in range(CHUNKS):
            cot_t[c, rows(i, LANES), :] = block[:, c * LANES:(c + 1) * LANES]

    for c in range(CHUNKS):
        mix_wait(tok_t, mixed, MIX, c)
        norm_in(c)
        gathers[c][0].start()
        gathers[c][1].start()
    w_up.wait_recv()
    transpose_up(up_far, 1)
    for c in range(CHUNKS):
        gathers[c][1].wait_recv()
        gathers[c][2].start()
    for c in range(CHUNKS):
        gathers[c][0].wait_recv()
        gathers[c][2].wait_recv()
        up(c)
    w_down.wait_recv()
    transpose_down(down_far, 1)
    for c in range(CHUNKS):
        down(c, 2)
        scatters[c][0].start()
        down(c, 0)
    for c in range(CHUNKS):
        scatters[c][0].wait_recv()
        add_near(part_f, near_f, pass_f, c)
        scatters[c][1].start()
    for c in range(CHUNKS):
        scatters[c][1].wait_recv()
        norm_out(c)
        gathers_b[c][0].start()
        gathers_b[c][1].start()
    for c in range(CHUNKS):
        write_out(c)
    for c in range(CHUNKS):
        gathers_b[c][1].wait_recv()
        gathers_b[c][2].start()
    for c in range(CHUNKS):
        gathers_b[c][0].wait_recv()
        gathers_b[c][2].wait_recv()
        if c == CHUNKS - 1:
            grad_down(1, gdown_out)
            g_down.start()
        hidden_back(c)
        shared_back(c, 2)
        scatters_b[c][0].start()
        shared_back(c, 0)
    grad_up(1, gup_out)
    g_up.start()
    for c in range(CHUNKS):
        scatters_b[c][0].wait_recv()
        add_near(part_b, near_b, pass_b, c)
        scatters_b[c][1].start()
    grad_down(0, gdown_ref)
    for c in range(CHUNKS):
        scatters_b[c][1].wait_recv()
        sum_back(c)
        mix_start(gsum16, mixed_back, MIX_BACK, c)
    grad_up(0, gup_ref)
    for c in range(CHUNKS):
        mix_wait(gsum16, mixed_back, MIX_BACK, c)
        tokens_back(c)
    g_down.wait_recv()
    gdown_ref[...] += gdown_in[...].astype(F32)
    g_up.wait_recv()
    gup_ref[...] += gup_in[...].astype(F32)
    for copy in [w_up, w_down, g_up, g_down]:
        copy.wait_send()
    for group in gathers + scatters + gathers_b + scatters_b:
        for copy in group:
            copy.wait_send()


def on_device(tokens, w_up, w_down, cotangent):
    count, _, width = tokens.shape
    own = w_up.shape[2]
    n_token = lax.axis_size("token")
    head = width // n_token
    samples = CHUNKS * WIDE
    vmem = pl.BlockSpec(memory_space=pltpu.VMEM)

    def blocks(dtype):
        return pltpu.VMEM((CHUNKS, width, LANES), dtype)

    def scatter_scratch():
        return [
            pltpu.VMEM((width, samples), BF16),
            pltpu.VMEM((CHUNKS, width, 2 * LANES), BF16),
            blocks(BF16),
            blocks(BF16),
        ]

    output, grad_tokens, grad_up, grad_down = pl.pallas_call(
        functools.partial(kernel, n_token, head),
        out_shape=(
            jax.ShapeDtypeStruct((count, width), BF16),
            jax.ShapeDtypeStruct((count, width), BF16),
            jax.ShapeDtypeStruct((width, own), F32),
            jax.ShapeDtypeStruct((own, width), F32),
        ),
        in_specs=[vmem] * 4,
        out_specs=(vmem,) * 4,
        scratch_shapes=[
            blocks(BF16), blocks(BF16), blocks(BF16),
            pltpu.VMEM((width, own), BF16), pltpu.VMEM((own, width), BF16),
            pltpu.VMEM((2 * own, width), BF16), pltpu.VMEM((width, 2 * own), BF16),
            pltpu.VMEM((width, samples), BF16),
            pltpu.VMEM((2 * own, samples), BF16), pltpu.VMEM((2 * own, samples), BF16),
            pltpu.VMEM((width, samples), BF16),
            pltpu.VMEM((2 * own, samples), BF16),
            *scatter_scratch(), *scatter_scratch(),
            blocks(F32), pltpu.VMEM((CHUNKS, 8, LANES), F32), blocks(F32), blocks(F32), blocks(BF16), blocks(BF16),
            pltpu.VMEM((width, own), BF16), pltpu.VMEM((width, own), BF16),
            pltpu.VMEM((own, width), BF16), pltpu.VMEM((own, width), BF16),
            pltpu.SemaphoreType.DMA((COPIES,)), pltpu.SemaphoreType.DMA((COPIES,)),
        ],
        compiler_params=pltpu.CompilerParams(
            collective_id=0, has_side_effects=True, vmem_limit_bytes=58 * 1024 * 1024
        ),
        name="rankmixer",
    )(tokens[:, 0], w_up[0], w_down[0], cotangent[:, 0])
    return output[:, None], grad_tokens[:, None], grad_up[None], grad_down[None]


def solution(mesh):
    specs = (
        P("dp", "token", None),
        P("token", None, "dp"),
        P("token", "dp", None),
    )
    in_specs = specs + (specs[0],)
    out_specs = (specs[0], specs[0], specs[1], specs[2])
    return jax.shard_map(
        on_device, mesh=mesh, in_specs=in_specs, out_specs=out_specs, check_vma=False
    )
```

time: 558 us -> 191 us (0.34)
  waiting for transfers between devices: 456 us -> 0 us
  Pallas kernels: 0 us -> 183 us
  matrix products: 31.9 us -> 0 us
  blocking collectives: 26.6 us -> 0 us
  other arithmetic: 16.5 us -> 0 us
  between operations: 13.9 us -> 0.65 us
  starting transfers between devices: 6.72 us -> 0 us
    reduce_scatter x2 -> x0, waiting for transfers between devices: 241 us -> none  [the longest x1 121 us: on_device(): lax.psum_scatter(jnp.einsum('spf,pdf->spd', grad_hidden, w_up, preferred_...]
    all_gather x2 -> x0, waiting for transfers between devices: 208 us -> none  [the longest x1 105 us: on_device(): all_shared = lax.all_gather(shared, 'dp', axis=0, tiled=True)]
    pallas_call x0 -> x1, Pallas kernels: none -> 183 us  [on_device(): pl.pallas_call(functools.partial(kernel, n_token, head), out_shape=(jax.S...]
    dot_general x6 -> x0, matrix products: 31.9 us -> none  [the longest x1 7.39 us: on_device(): jnp.einsum('spd,pfd->spf', grad_ffn, w_down, preferred_element_type=jnp.f...]
    all_to_all x1 -> x0, blocking collectives: 26.6 us -> none  [on_device(): lax.all_to_all(split_heads, 'token', split_axis=2, concat_axis=1, tiled=T...]
    convert_element_type x4 -> x0, other arithmetic: 8.9 us -> none  [the longest x1 2.93 us: on_device(): grad_out.astype(jnp.bfloat16)]
    reduce_sum x6 -> x0, other arithmetic: 7.55 us -> none  [the longest x2 3.45 us: norm_back(): first = jnp.mean(upstream, axis=-1, keepdims=True)]
    all_to_all x1 -> x0, starting transfers between devices: 6.37 us -> none  [on_device(): lax.all_to_all(back_heads, 'token', split_axis=2, concat_axis=1, tiled=True)]
  transfers between devices with their start and end apart: 5 -> 0, of which waited for: 5 -> 0; matrix products, arithmetic and copies ran while one was open for 2% -> 0% of each run, Pallas kernels for 0% -> 0%
where the time goes in v2:
time: 191 us
  Pallas kernels  183 us (96%)
  local copies, waits for them, and re-layouts  7.55 us (4%)
    pallas_call x1, Pallas kernels, on_device(): pl.pallas_call(functools.partial(kernel, n_token, head), out_shape=(jax.S...  183 us
    unnamed x8, local copies, waits for them, and re-layouts  7.55 us

profile of v2, /device:TPU:1, one launch (start us, length us, event | category | flops | bytes accessed | tf_op | source)
XLA Modules:
  0.0 190.9 jit_solution(9898276459131871782)
XLA Ops:
  0.6 182.7 %rankmixer.1 = (bf16[256,1024]{1,0:T(8,128)(2,1)}, bf16[256,1024]{1,0:T(8,128)(2,1)}, f32[1024,512]{1,0:T(8,128)}, f32[512,1024]{1,0:T(8,128)}) custom-call(bf16[256,1024]{1,0:T(8,128)(2,1)} %bitcast.14, bf16[1024,512]{1,0:T(8,128)(2,1)} %bitcast.10, bf16[512,1024]{1,0:T(8,128)(2,1)} %bitcast.11, bf16[256,1024]{1,0:T(8,128)(2,1)} %bitcast.15), custom_call_target="tpu_custom_call" | custom-call | tf_op jit(solution)/shard_map/rankmixer/pallas_call | solution.py:350
  183.4 0.0 copy-start.1
  183.4 2.0 %copy.12 = bf16[256,1,1024]{2,0,1:T(8,128)(2,1)} copy(bf16[256,1,1024]{2,0,1:T(8,128)(2,1)} %bitcast.13) | data formatting | bytes 1048576
  185.4 1.9 copy.13
  187.2 0.0 copy-done.1
  187.2 0.0 copy-start
  187.3 1.3 copy.14
  188.6 1.0 copy-done
  189.6 1.3 copy.15
Async XLA Ops:
  183.4 3.9 %copy-start.1 = (f32[1024,512]{1,0:T(8,128)S(1)}, f32[1024,512]{1,0:T(8,128)}, u32[]{:S(2)}) copy-start(f32[1024,512]{1,0:T(8,128)} %get-tuple-element.10) | copy-start | bytes 6291460
  187.2 2.3 %copy-start = (f32[512,1024]{1,0:T(8,128)S(1)}, f32[512,1024]{1,0:T(8,128)}, u32[]{:S(2)}) copy-start(f32[512,1024]{1,0:T(8,128)} %get-tuple-element.11) | copy-start | bytes 6291460

commit v3 on v2

--- a/solution.py
+++ b/solution.py
@@ -17,9 +17,16 @@
 F32 = jnp.float32
 BF16 = jnp.bfloat16
 
-MIX, MIX_BACK, UP, DOWN, GRAD_UP, GRAD_DOWN = 0, 2, 4, 5, 6, 7
-GATHER, SCATTER, GATHER_BACK, SCATTER_BACK = 8, 14, 18, 24
-COPIES = 28
+BLOCKS = 4
+
+SPAN = CHUNKS * BLOCKS
+MIX, MIX_BACK, UP, GRAD_DOWN, NEAR_Y, NEAR_Y_BACK, SHARED, HIDDEN = 0, 2, 4, 5, 6, 8, 10, 12
+DOWN = 14
+GATHER = DOWN + BLOCKS
+SCATTER = GATHER + 2 * SPAN
+GATHER_BACK = SCATTER + 2 * SPAN
+SCATTER_BACK = GATHER_BACK + 2 * SPAN
+COPIES = SCATTER_BACK + 2 * SPAN
 
 
 def dot_nn(a, b):
@@ -58,9 +65,9 @@
     out_ref, gtok_ref, gup_ref, gdown_ref,
     tok_t, mixed, cot_t, up_far, down_far, up_t, down_t,
     shared, activ, slope, gffn, ghid,
-    part_f, near_f, pass_f, far_f, part_b, near_b, pass_b, far_b,
+    part_f, near_f, passed_f, far_f, part_b, near_b, passed_b, far_b,
     normed, scale_in, gout, gsum, gsum16, mixed_back,
-    gup_out, gup_in, gdown_out, gdown_in,
+    shared_far, ghid_far, gdown_out, gdown_in,
     send, recv,
 ):
     dp = lax.axis_index("dp")
@@ -77,11 +84,14 @@
             device_id=device, device_id_type=MESH,
         )
 
-    def piece(ref, c, p, n=1):
-        return ref.at[:, pl.ds(c * WIDE + p * LANES, n * LANES)]
+    block = d_model // BLOCKS
 
     def rows(i, n):
-        return pl.ds(pl.multiple_of(i * n, n), n)
+        return pl.ds(i * n if isinstance(i, int) else pl.multiple_of(i * n, n), n)
+
+    def piece(ref, c, p, n=1, q=None):
+        r = slice(None) if q is None else rows(q, block)
+        return ref.at[r, pl.ds(c * WIDE + p * LANES, n * LANES)]
 
     barrier = pltpu.get_barrier_semaphore()
 
@@ -100,8 +110,23 @@
 
     pl.semaphore_wait(barrier, n_token + 2)
 
-    w_up = remote(up_ref, up_far, UP, dev_w)
-    w_down = remote(down_ref, down_far, DOWN, dev_w)
+    def w_up():
+        return remote(up_ref, up_far, UP, dev_w)
+
+    def w_down(q):
+        r = rows(q, block)
+        return remote(down_ref.at[:, r], down_far.at[:, r], DOWN + q, dev_w)
+
+    def shared_on(c):
+        span = pl.ds(c * WIDE, WIDE)
+        return remote(shared.at[:, span], shared_far.at[:, span], SHARED + c, dev_w)
+
+    def hidden_on(c):
+        span = pl.ds(c * WIDE, WIDE)
+        return remote(ghid.at[pl.ds(own, own), span], ghid_far.at[:, span], HIDDEN + c, dev_w)
+
+    def g_down():
+        return remote(gdown_out, gdown_in, GRAD_DOWN, dev_w)
 
     def mix_start(src, dst, sem, c):
         @pl.loop(1, n_token)
@@ -119,35 +144,34 @@
         whole.wait_send()
         whole.wait_recv()
 
-    def gather(ref, sem, c):
-        return (
-            remote(piece(ref, c, 0), piece(ref, c, 2), sem + c, dev_y),
-            remote(piece(ref, c, 0), piece(ref, c, 1), sem + 2 + c, dev_z),
-            remote(piece(ref, c, 1), piece(ref, c, 3), sem + 4 + c, dev_y),
-        )
-
-    def scatter(part, near, passed, far, sem, c):
-        return (
-            remote(piece(part, c, 2, 2), near.at[c], sem + c, dev_y),
-            remote(passed.at[c], far.at[c], sem + 2 + c, dev_z),
-        )
-
-    gathers = [gather(shared, GATHER, c) for c in range(CHUNKS)]
-    scatters = [scatter(part_f, near_f, pass_f, far_f, SCATTER, c) for c in range(CHUNKS)]
-    gathers_b = [gather(gffn, GATHER_BACK, c) for c in range(CHUNKS)]
-    scatters_b = [scatter(part_b, near_b, pass_b, far_b, SCATTER_BACK, c) for c in range(CHUNKS)]
-    g_up = remote(gup_out, gup_in, GRAD_UP, dev_w)
-    g_down = remote(gdown_out, gdown_in, GRAD_DOWN, dev_w)
+    def gather_y(ref, sem, c):
+        return remote(piece(ref, c, 0), piece(ref, c, 2), sem + c, dev_y)
+
+    def gather_z(ref, sem, c, q):
+        return remote(piece(ref, c, 0, 1, q), piece(ref, c, 1, 1, q), sem + c * BLOCKS + q, dev_z)
+
+    def gather_on(ref, sem, c, q):
+        return remote(piece(ref, c, 1, 1, q), piece(ref, c, 3, 1, q), sem + SPAN + c * BLOCKS + q, dev_y)
+
+    def scatter_y(part, near, sem, c, q):
+        return remote(piece(part, c, 2, 2, q), near.at[c, rows(q, block), :], sem + c * BLOCKS + q, dev_y)
+
+    def scatter_z(passed, far, sem, c, q):
+        r = rows(q, block)
+        return remote(passed.at[c, r, :], far.at[c, r, :], sem + SPAN + c * BLOCKS + q, dev_z)
+
+    def each_block(step):
+        pl.loop(0, BLOCKS)(step)
 
     def transpose_up(src, half):
         @pl.loop(0, own // LANES)
         def _(i):
             up_t[pl.ds(pl.multiple_of(half * own + i * LANES, LANES), LANES), :] = src[:, rows(i, LANES)].T
 
-    def transpose_down(src, half):
-        @pl.loop(0, d_model // LANES)
-        def _(i):
-            down_t[rows(i, LANES), pl.ds(half * own, own)] = src[:, rows(i, LANES)].T
+    def transpose_down(src, half, q):
+        for i in range(block // LANES):
+            r = pl.ds(q * block + i * LANES, LANES)
+            down_t[r, pl.ds(half * own, own)] = src[:, r].T
 
     def norm_in(c):
         summed = mixed[c].astype(F32) + tok_t[c].astype(F32)
@@ -167,18 +191,21 @@
             activ[r, span] = value.astype(BF16)
             slope[r, span] = grade.astype(BF16)
 
-    def down(c, p):
-        span = pl.ds(c * WIDE + p * LANES, 2 * LANES)
-
-        @pl.loop(0, d_model // MXU_ROWS)
-        def _(i):
-            r = rows(i, MXU_ROWS)
+    def down(c, q):
+        r = rows(q, block)
+        for p in (2, 0):
+            span = pl.ds(c * WIDE + p * LANES, 2 * LANES)
             part_f[r, span] = dot_nn(down_t[r, :], activ[:, span]).astype(BF16)
-
-    def add_near(part, near, passed, c):
-        passed[c] = (
-            part[:, c * WIDE + LANES:c * WIDE + 2 * LANES].astype(F32) + near[c, :, LANES:].astype(F32)
+            if p == 2:
+                scatter_y(part_f, near_f, SCATTER, c, q).start()
+
+    def pass_on(part, near, passed, far, sem, c, q):
+        r = rows(q, block)
+        scatter_y(part, near, sem, c, q).wait_recv()
+        passed[c, r, :] = (
+            part[r, c * WIDE + LANES:c * WIDE + 2 * LANES].astype(F32) + near[c, r, LANES:].astype(F32)
         ).astype(BF16)
+        scatter_z(passed, far, sem, c, q).start()
 
     def total(part, near, far, c):
         return (
@@ -209,16 +236,16 @@
                 grad = dot_nn(src[rows(i, MXU_ROWS), :], gffn[:, span])
                 ghid[r, span] = (grad * slope[r, span].astype(F32)).astype(BF16)
 
-    def shared_back(c, p):
-        span = pl.ds(c * WIDE + p * LANES, 2 * LANES)
-
-        @pl.loop(0, d_model // MXU_ROWS)
-        def _(i):
-            r = rows(i, MXU_ROWS)
+    def shared_back(c, q):
+        r = rows(q, block)
+        for p in (2, 0):
+            span = pl.ds(c * WIDE + p * LANES, 2 * LANES)
             part_b[r, span] = (
                 dot_nn(up_ref[r, :], ghid[pl.ds(0, own), span])
                 + dot_nn(up_far[r, :], ghid[pl.ds(own, own), span])
             ).astype(BF16)
+            if p == 2:
+                scatter_y(part_b, near_b, SCATTER_BACK, c, q).start()
 
     def sum_back(c):
         grad = total(part_b, near_b, far_b, c) + gout[c]
@@ -239,93 +266,162 @@
             r = pl.ds(pl.multiple_of(half * own + i * MXU_ROWS, MXU_ROWS), MXU_ROWS)
             dst[rows(i, MXU_ROWS), :] = dot_nt(activ[r, :], gffn[...]).astype(dst.dtype)
 
-    def grad_up(half, dst):
+    def grad_up():
         @pl.loop(0, d_model // MXU_ROWS)
         def _(i):
             r = rows(i, MXU_ROWS)
-            dst[r, :] = dot_nt(shared[r, :], ghid[pl.ds(half * own, own), :]).astype(dst.dtype)
+            gup_ref[r, :] = dot_nt(shared[r, :], ghid[pl.ds(0, own), :]) + dot_nt(
+                shared_far[r, pl.ds(0, WIDE)], ghid_far[:, pl.ds(0, WIDE)]
+            )
+
+    def grad_up_end():
+        @pl.loop(0, d_model // MXU_ROWS)
+        def _(i):
+            r = rows(i, MXU_ROWS)
+            gup_ref[r, :] += dot_nt(shared_far[r, pl.ds(WIDE, WIDE)], ghid_far[:, pl.ds(WIDE, WIDE)])
 
     for c in range(CHUNKS):
         mix_start(tok_t, mixed, MIX, c)
-    w_up.start()
-    w_down.start()
+    w_up().start()
+    for q in range(BLOCKS):
+        w_down(q).start()
     transpose_up(up_ref, 0)
-    transpose_down(down_ref, 0)
+    for q in range(BLOCKS):
+        transpose_down(down_ref, 0, q)
 
     @pl.loop(0, d_model // LANES)
     def _(i):
-        block = cot_ref[:, rows(i, LANES)].T
+        tile = cot_ref[:, rows(i, LANES)].T
         for c in range(CHUNKS):
-            cot_t[c, rows(i, LANES), :] = block[:, c * LANES:(c + 1) * LANES]
-
+            cot_t[c, rows(i, LANES), :] = tile[:, c * LANES:(c + 1) * LANES]
+
+    mix_wait(tok_t, mixed, MIX, 0)
+    norm_in(0)
+    gather_y(shared, NEAR_Y, 0).start()
+    mix_wait(tok_t, mixed, MIX, 1)
+    each_block(lambda q: gather_z(shared, GATHER, 0, q).start())
+    norm_in(1)
+    gather_y(shared, NEAR_Y, 1).start()
+
+    def gather_turn(ref, sem):
+        def step(q):
+            gather_z(ref, sem, 0, q).wait_recv()
+            gather_on(ref, sem, 0, q).start()
+            gather_z(ref, sem, 1, q).start()
+
+        each_block(step)
+
+    def gather_end(ref, sem, near, c):
+        gather_y(ref, near, c).wait_recv()
+        each_block(lambda q: gather_on(ref, sem, c, q).wait_recv())
+
+    def forward_on(ref, sem, q):
+        gather_z(ref, sem, 1, q).wait_recv()
+        gather_on(ref, sem, 1, q).start()
+
+    def down_block(q):
+        w_down(q).wait_recv()
+        transpose_down(down_far, 1, q)
+        down(0, q)
+
+    def pass_f(c, q):
+        pass_on(part_f, near_f, passed_f, far_f, SCATTER, c, q)
+
+    def pass_b(c, q):
+        pass_on(part_b, near_b, passed_b, far_b, SCATTER_BACK, c, q)
+
+    gather_turn(shared, GATHER)
+    w_up().wait_recv()
+    transpose_up(up_far, 1)
+    gather_end(shared, GATHER, NEAR_Y, 0)
+    shared_on(0).start()
+    up(0)
+    down_block(0)
+    forward_on(shared, GATHER, 0)
+    forward_on(shared, GATHER, 1)
+    down_block(1)
+    forward_on(shared, GATHER, 2)
+    forward_on(shared, GATHER, 3)
+    pass_f(0, 0)
+    gather_end(shared, GATHER, NEAR_Y, 1)
+    shared_on(1).start()
+    up(1)
+    pass_f(0, 1)
+    down_block(2)
+    down(1, 0)
+    down(1, 1)
+    pass_f(0, 2)
+    down(1, 2)
+    down_block(3)
+    pass_f(1, 0)
+    down(1, 3)
+    pass_f(0, 3)
+    pass_f(1, 1)
+    pass_f(1, 2)
+    pass_f(1, 3)
+    each_block(lambda q: scatter_z(passed_f, far_f, SCATTER, 0, q).wait_recv())
+    norm_out(0)
+    gather_y(gffn, NEAR_Y_BACK, 0).start()
+    each_block(lambda q: gather_z(gffn, GATHER_BACK, 0, q).start())
+    each_block(lambda q: scatter_z(passed_f, far_f, SCATTER, 1, q).wait_recv())
+    norm_out(1)
+    gather_y(gffn, NEAR_Y_BACK, 1).start()
+    write_out(0)
+    gather_turn(gffn, GATHER_BACK)
+    write_out(1)
+    gather_end(gffn, GATHER_BACK, NEAR_Y_BACK, 0)
+    hidden_back(0)
+    hidden_on(0).start()
+
+    def back_block(q):
+        shared_back(0, q)
+        forward_on(gffn, GATHER_BACK, q)
+
+    each_block(back_block)
+    each_block(lambda q: pass_b(0, q))
+    gather_end(gffn, GATHER_BACK, NEAR_Y_BACK, 1)
+    grad_down(1, gdown_out)
+    g_down().start()
+    hidden_back(1)
+    hidden_on(1).start()
+    each_block(lambda q: shared_back(1, q))
+    each_block(lambda q: pass_b(1, q))
+    each_block(lambda q: scatter_z(passed_b, far_b, SCATTER_BACK, 0, q).wait_recv())
+    sum_back(0)
+    mix_start(gsum16, mixed_back, MIX_BACK, 0)
+    grad_down(0, gdown_ref)
+    each_block(lambda q: scatter_z(passed_b, far_b, SCATTER_BACK, 1, q).wait_recv())
+    sum_back(1)
+    mix_start(gsum16, mixed_back, MIX_BACK, 1)
     for c in range(CHUNKS):
-        mix_wait(tok_t, mixed, MIX, c)
-        norm_in(c)
-        gathers[c][0].start()
-        gathers[c][1].start()
-    w_up.wait_recv()
-    transpose_up(up_far, 1)
-    for c in range(CHUNKS):
-        gathers[c][1].wait_recv()
-        gathers[c][2].start()
-    for c in range(CHUNKS):
-        gathers[c][0].wait_recv()
-        gathers[c][2].wait_recv()
-        up(c)
-    w_down.wait_recv()
-    transpose_down(down_far, 1)
-    for c in range(CHUNKS):
-        down(c, 2)
-        scatters[c][0].start()
-        down(c, 0)
-    for c in range(CHUNKS):
-        scatters[c][0].wait_recv()
-        add_near(part_f, near_f, pass_f, c)
-        scatters[c][1].start()
-    for c in range(CHUNKS):
-        scatters[c][1].wait_recv()
-        norm_out(c)
-        gathers_b[c][0].start()
-        gathers_b[c][1].start()
-    for c in range(CHUNKS):
-        write_out(c)
-    for c in range(CHUNKS):
-        gathers_b[c][1].wait_recv()
-        gathers_b[c][2].start()
-    for c in range(CHUNKS):
-        gathers_b[c][0].wait_recv()
-        gathers_b[c][2].wait_recv()
-        if c == CHUNKS - 1:
-            grad_down(1, gdown_out)
-            g_down.start()
-        hidden_back(c)
-        shared_back(c, 2)
-        scatters_b[c][0].start()
-        shared_back(c, 0)
-    grad_up(1, gup_out)
-    g_up.start()
-    for c in range(CHUNKS):
-        scatters_b[c][0].wait_recv()
-        add_near(part_b, near_b, pass_b, c)
-        scatters_b[c][1].start()
-    grad_down(0, gdown_ref)
-    for c in range(CHUNKS):
-        scatters_b[c][1].wait_recv()
-        sum_back(c)
-        mix_start(gsum16, mixed_back, MIX_BACK, c)
-    grad_up(0, gup_ref)
+        shared_on(c).wait_recv()
+    hidden_on(0).wait_recv()
+    grad_up()
     for c in range(CHUNKS):
         mix_wait(gsum16, mixed_back, MIX_BACK, c)
         tokens_back(c)
-    g_down.wait_recv()
+    g_down().wait_recv()
     gdown_ref[...] += gdown_in[...].astype(F32)
-    g_up.wait_recv()
-    gup_ref[...] += gup_in[...].astype(F32)
-    for copy in [w_up, w_down, g_up, g_down]:
+    hidden_on(1).wait_recv()
+    grad_up_end()
+    for copy in [w_up(), g_down(), shared_on(0), shared_on(1), hidden_on(0), hidden_on(1)]:
         copy.wait_send()
-    for group in gathers + scatters + gathers_b + scatters_b:
-        for copy in group:
-            copy.wait_send()
+    each_block(lambda q: w_down(q).wait_send())
+    for c in range(CHUNKS):
+        gather_y(shared, NEAR_Y, c).wait_send()
+        gather_y(gffn, NEAR_Y_BACK, c).wait_send()
+
+        def drain(q):
+            gather_z(shared, GATHER, c, q).wait_send()
+            gather_on(shared, GATHER, c, q).wait_send()
+            scatter_y(part_f, near_f, SCATTER, c, q).wait_send()
+            scatter_z(passed_f, far_f, SCATTER, c, q).wait_send()
+            gather_z(gffn, GATHER_BACK, c, q).wait_send()
+            gather_on(gffn, GATHER_BACK, c, q).wait_send()
+            scatter_y(part_b, near_b, SCATTER_BACK, c, q).wait_send()
+            scatter_z(passed_b, far_b, SCATTER_BACK, c, q).wait_send()
+
+        each_block(drain)
 
 
 def on_device(tokens, w_up, w_down, cotangent):
@@ -367,7 +463,7 @@
             pltpu.VMEM((2 * own, samples), BF16),
             *scatter_scratch(), *scatter_scratch(),
             blocks(F32), pltpu.VMEM((CHUNKS, 8, LANES), F32), blocks(F32), blocks(F32), blocks(BF16), blocks(BF16),
-            pltpu.VMEM((width, own), BF16), pltpu.VMEM((width, own), BF16),
+            pltpu.VMEM((width, samples), BF16), pltpu.VMEM((own, samples), BF16),
             pltpu.VMEM((own, width), BF16), pltpu.VMEM((own, width), BF16),
             pltpu.SemaphoreType.DMA((COPIES,)), pltpu.SemaphoreType.DMA((COPIES,)),
         ],

time: 191 us -> 180 us (0.942); the launches traced: 191 us -> 178 us
  Pallas kernels: 183 us -> 169 us
    pallas_call x1, Pallas kernels: 183 us -> 169 us  [on_device(): pl.pallas_call(functools.partial(kernel, n_token, head), out_shape=(jax.S...]
where the time goes in v3:
time: 180 us; the launch traced here: 178 us
  Pallas kernels  169 us (94%)
  local copies, waits for them, and re-layouts  7.55 us (4%)
    pallas_call x1, Pallas kernels, on_device(): pl.pallas_call(functools.partial(kernel, n_token, head), out_shape=(jax.S...  169 us
    unnamed x8, local copies, waits for them, and re-layouts  7.55 us

profile of v3, /device:TPU:1, one launch (start us, length us, event | category | flops | bytes accessed | tf_op | source)
XLA Modules:
  0.0 177.6 jit_solution(15903331106862548778)
XLA Ops:
  0.6 169.3 %rankmixer.1 = (bf16[256,1024]{1,0:T(8,128)(2,1)}, bf16[256,1024]{1,0:T(8,128)(2,1)}, f32[1024,512]{1,0:T(8,128)}, f32[512,1024]{1,0:T(8,128)}) custom-call(bf16[256,1024]{1,0:T(8,128)(2,1)} %bitcast.14, bf16[1024,512]{1,0:T(8,128)(2,1)} %bitcast.10, bf16[512,1024]{1,0:T(8,128)(2,1)} %bitcast.11, bf16[256,1024]{1,0:T(8,128)(2,1)} %bitcast.15), custom_call_target="tpu_custom_call" | custom-call | tf_op jit(solution)/shard_map/rankmixer/pallas_call | solution.py:446
  170.0 0.0 copy-start.1
  170.0 2.0 %copy.12 = bf16[256,1,1024]{2,0,1:T(8,128)(2,1)} copy(bf16[256,1,1024]{2,0,1:T(8,128)(2,1)} %bitcast.13) | data formatting | bytes 1048576
  172.0 1.9 %copy.13 = bf16[256,1,1024]{2,0,1:T(8,128)(2,1)} copy(bf16[256,1,1024]{2,0,1:T(8,128)(2,1)} %bitcast.12) | data formatting | bytes 1048576
  173.9 0.0 copy-done.1
  173.9 0.0 copy-start
  173.9 1.3 copy.14
  175.2 1.0 copy-done
  176.2 1.3 copy.15
Async XLA Ops:
  170.0 3.9 %copy-start.1 = (f32[1024,512]{1,0:T(8,128)S(1)}, f32[1024,512]{1,0:T(8,128)}, u32[]{:S(2)}) copy-start(f32[1024,512]{1,0:T(8,128)} %get-tuple-element.10) | copy-start | bytes 6291460
  173.9 2.3 %copy-start = (f32[512,1024]{1,0:T(8,128)S(1)}, f32[512,1024]{1,0:T(8,128)}, u32[]{:S(2)}) copy-start(f32[512,1024]{1,0:T(8,128)} %get-tuple-element.11) | copy-start | bytes 6291460

commit v4 on v3

--- a/solution.py
+++ b/solution.py
@@ -334,31 +334,22 @@
     w_up().wait_recv()
     transpose_up(up_far, 1)
     gather_end(shared, GATHER, NEAR_Y, 0)
+    up(0)
+    for q in range(BLOCKS - 1):
+        down_block(q)
+        forward_on(shared, GATHER, q)
+    pass_f(0, 0)
+    down_block(3)
+    forward_on(shared, GATHER, 3)
     shared_on(0).start()
-    up(0)
-    down_block(0)
-    forward_on(shared, GATHER, 0)
-    forward_on(shared, GATHER, 1)
-    down_block(1)
-    forward_on(shared, GATHER, 2)
-    forward_on(shared, GATHER, 3)
-    pass_f(0, 0)
+    pass_f(0, 1)
+    pass_f(0, 2)
     gather_end(shared, GATHER, NEAR_Y, 1)
     shared_on(1).start()
+    pass_f(0, 3)
     up(1)
-    pass_f(0, 1)
-    down_block(2)
-    down(1, 0)
-    down(1, 1)
-    pass_f(0, 2)
-    down(1, 2)
-    down_block(3)
-    pass_f(1, 0)
-    down(1, 3)
-    pass_f(0, 3)
-    pass_f(1, 1)
-    pass_f(1, 2)
-    pass_f(1, 3)
+    each_block(lambda q: down(1, q))
+    each_block(lambda q: pass_f(1, q))
     each_block(lambda q: scatter_z(passed_f, far_f, SCATTER, 0, q).wait_recv())
     norm_out(0)
     gather_y(gffn, NEAR_Y_BACK, 0).start()
@@ -380,15 +371,16 @@
     each_block(back_block)
     each_block(lambda q: pass_b(0, q))
     gather_end(gffn, GATHER_BACK, NEAR_Y_BACK, 1)
-    grad_down(1, gdown_out)
-    g_down().start()
     hidden_back(1)
     hidden_on(1).start()
     each_block(lambda q: shared_back(1, q))
-    each_block(lambda q: pass_b(1, q))
+    grad_down(1, gdown_out)
+    g_down().start()
+    pass_b(1, 0)
     each_block(lambda q: scatter_z(passed_b, far_b, SCATTER_BACK, 0, q).wait_recv())
     sum_back(0)
     mix_start(gsum16, mixed_back, MIX_BACK, 0)
+    pl.loop(1, BLOCKS)(lambda q: pass_b(1, q))
     grad_down(0, gdown_ref)
     each_block(lambda q: scatter_z(passed_b, far_b, SCATTER_BACK, 1, q).wait_recv())
     sum_back(1)
@@ -397,13 +389,13 @@
         shared_on(c).wait_recv()
     hidden_on(0).wait_recv()
     grad_up()
+    hidden_on(1).wait_recv()
+    grad_up_end()
+    g_down().wait_recv()
+    gdown_ref[...] += gdown_in[...].astype(F32)
     for c in range(CHUNKS):
         mix_wait(gsum16, mixed_back, MIX_BACK, c)
         tokens_back(c)
-    g_down().wait_recv()
-    gdown_ref[...] += gdown_in[...].astype(F32)
-    hidden_on(1).wait_recv()
-    grad_up_end()
     for copy in [w_up(), g_down(), shared_on(0), shared_on(1), hidden_on(0), hidden_on(1)]:
         copy.wait_send()
     each_block(lambda q: w_down(q).wait_send())
@@ -446,10 +438,10 @@
     output, grad_tokens, grad_up, grad_down = pl.pallas_call(
         functools.partial(kernel, n_token, head),
         out_shape=(
-            jax.ShapeDtypeStruct((count, width), BF16),
-            jax.ShapeDtypeStruct((count, width), BF16),
-            jax.ShapeDtypeStruct((width, own), F32),
-            jax.ShapeDtypeStruct((own, width), F32),
+            pltpu.VMEM((count, width), BF16),
+            pltpu.VMEM((count, width), BF16),
+            pltpu.VMEM((width, own), F32),
+            pltpu.VMEM((own, width), F32),
         ),
         in_specs=[vmem] * 4,
         out_specs=(vmem,) * 4,
@@ -468,7 +460,7 @@
             pltpu.SemaphoreType.DMA((COPIES,)), pltpu.SemaphoreType.DMA((COPIES,)),
         ],
         compiler_params=pltpu.CompilerParams(
-            collective_id=0, has_side_effects=True, vmem_limit_bytes=58 * 1024 * 1024
+            collective_id=0, has_side_effects=True, vmem_limit_bytes=50 * 1024 * 1024
         ),
         name="rankmixer",
     )(tokens[:, 0], w_up[0], w_down[0], cotangent[:, 0])

time: 180 us -> 169 us (0.939)
  the two profiles are of different devices: /device:TPU:1 before, /device:TPU:230 now
where the time goes in v4:
time: 169 us
  Pallas kernels  164 us (97%)
  local copies, waits for them, and re-layouts  4.23 us (3%)
    pallas_call x1, Pallas kernels, on_device(): pl.pallas_call(functools.partial(kernel, n_token, head), out_shape=(pltpu...  164 us
    unnamed x4, local copies, waits for them, and re-layouts  4.23 us

profile of v4, /device:TPU:230, one launch (start us, length us, event | category | flops | bytes accessed | tf_op | source)
XLA Modules:
  0.0 169.3 jit_solution(13022972223125497010)
XLA Ops:
  0.6 164.5 %rankmixer.1 = (bf16[256,1024]{1,0:T(8,128)(2,1)S(1)}, bf16[256,1024]{1,0:T(8,128)(2,1)S(1)}, f32[1024,512]{1,0:T(8,128)S(1)}, f32[512,1024]{1,0:T(8,128)S(1)}) custom-call(bf16[256,1024]{1,0:T(8,128)(2,1)} %bitcast.14, bf16[1024,512]{1,0:T(8,128)(2,1)} %bitcast.12, bf16[512,1024]{1,0:T(8,128)(2,1)} %bitcast.13, bf16[256,1024]{1,0:T(8,128)(2,1)} %bitcast.15), custom_call_target="tpu_custom_call" | custom-call | tf_op jit(solution)/shard_map/rankmixer/pallas_call | solution.py:438
  165.1 0.8 copy.12
  165.9 0.8 copy.13
  166.7 1.3 copy.14
  168.0 1.3 copy.15

commit v5 on v4

--- a/solution.py
+++ b/solution.py
@@ -21,7 +21,8 @@
 
 SPAN = CHUNKS * BLOCKS
 MIX, MIX_BACK, UP, GRAD_DOWN, NEAR_Y, NEAR_Y_BACK, SHARED, HIDDEN = 0, 2, 4, 5, 6, 8, 10, 12
-DOWN = 14
+SCATTER_OWN, SCATTER_OWN_BACK = 14, 16
+DOWN = 18
 GATHER = DOWN + BLOCKS
 SCATTER = GATHER + 2 * SPAN
 GATHER_BACK = SCATTER + 2 * SPAN
@@ -154,7 +155,11 @@
         return remote(piece(ref, c, 1, 1, q), piece(ref, c, 3, 1, q), sem + SPAN + c * BLOCKS + q, dev_y)
 
     def scatter_y(part, near, sem, c, q):
-        return remote(piece(part, c, 2, 2, q), near.at[c, rows(q, block), :], sem + c * BLOCKS + q, dev_y)
+        r = rows(q, block)
+        return remote(piece(part, c, 3, 1, q), near.at[c, r, pl.ds(LANES, LANES)], sem + c * BLOCKS + q, dev_y)
+
+    def scatter_own(part, near, sem, c):
+        return remote(piece(part, c, 2), near.at[c, :, pl.ds(0, LANES)], sem + c, dev_y)
 
     def scatter_z(passed, far, sem, c, q):
         r = rows(q, block)
@@ -307,9 +312,12 @@
         def step(q):
             gather_z(ref, sem, 0, q).wait_recv()
             gather_on(ref, sem, 0, q).start()
-            gather_z(ref, sem, 1, q).start()
+            if sem != GATHER:
+                gather_z(ref, sem, 1, q).start()
 
         each_block(step)
+        if sem == GATHER:
+            each_block(lambda q: gather_z(ref, sem, 1, q).start())
 
     def gather_end(ref, sem, near, c):
         gather_y(ref, near, c).wait_recv()
@@ -340,6 +348,7 @@
         forward_on(shared, GATHER, q)
     pass_f(0, 0)
     down_block(3)
+    scatter_own(part_f, near_f, SCATTER_OWN, 0).start()
     forward_on(shared, GATHER, 3)
     shared_on(0).start()
     pass_f(0, 1)
@@ -349,12 +358,15 @@
     pass_f(0, 3)
     up(1)
     each_block(lambda q: down(1, q))
+    scatter_own(part_f, near_f, SCATTER_OWN, 1).start()
     each_block(lambda q: pass_f(1, q))
     each_block(lambda q: scatter_z(passed_f, far_f, SCATTER, 0, q).wait_recv())
+    scatter_own(part_f, near_f, SCATTER_OWN, 0).wait_recv()
     norm_out(0)
     gather_y(gffn, NEAR_Y_BACK, 0).start()
     each_block(lambda q: gather_z(gffn, GATHER_BACK, 0, q).start())
     each_block(lambda q: scatter_z(passed_f, far_f, SCATTER, 1, q).wait_recv())
+    scatter_own(part_f, near_f, SCATTER_OWN, 1).wait_recv()
     norm_out(1)
     gather_y(gffn, NEAR_Y_BACK, 1).start()
     write_out(0)
@@ -369,20 +381,24 @@
         forward_on(gffn, GATHER_BACK, q)
 
     each_block(back_block)
+    scatter_own(part_b, near_b, SCATTER_OWN_BACK, 0).start()
     each_block(lambda q: pass_b(0, q))
     gather_end(gffn, GATHER_BACK, NEAR_Y_BACK, 1)
     hidden_back(1)
     hidden_on(1).start()
     each_block(lambda q: shared_back(1, q))
+    scatter_own(part_b, near_b, SCATTER_OWN_BACK, 1).start()
     grad_down(1, gdown_out)
     g_down().start()
     pass_b(1, 0)
     each_block(lambda q: scatter_z(passed_b, far_b, SCATTER_BACK, 0, q).wait_recv())
+    scatter_own(part_b, near_b, SCATTER_OWN_BACK, 0).wait_recv()
     sum_back(0)
     mix_start(gsum16, mixed_back, MIX_BACK, 0)
     pl.loop(1, BLOCKS)(lambda q: pass_b(1, q))
     grad_down(0, gdown_ref)
     each_block(lambda q: scatter_z(passed_b, far_b, SCATTER_BACK, 1, q).wait_recv())
+    scatter_own(part_b, near_b, SCATTER_OWN_BACK, 1).wait_recv()
     sum_back(1)
     mix_start(gsum16, mixed_back, MIX_BACK, 1)
     for c in range(CHUNKS):
@@ -402,6 +418,8 @@
     for c in range(CHUNKS):
         gather_y(shared, NEAR_Y, c).wait_send()
         gather_y(gffn, NEAR_Y_BACK, c).wait_send()
+        scatter_own(part_f, near_f, SCATTER_OWN, c).wait_send()
+        scatter_own(part_b, near_b, SCATTER_OWN_BACK, c).wait_send()
 
         def drain(q):
             gather_z(shared, GATHER, c, q).wait_send()

time: 169 us -> 163 us (0.964)
  the two profiles are of different devices: /device:TPU:230 before, /device:TPU:1 now
where the time goes in v5:
time: 163 us; the launch traced here: 162 us
  Pallas kernels  158 us (97%)
  local copies, waits for them, and re-layouts  4.23 us (3%)
    pallas_call x1, Pallas kernels, on_device(): pl.pallas_call(functools.partial(kernel, n_token, head), out_shape=(pltpu...  158 us
    unnamed x4, local copies, waits for them, and re-layouts  4.23 us

profile of v5, /device:TPU:1, one launch (start us, length us, event | category | flops | bytes accessed | tf_op | source)
XLA Modules:
  0.0 162.5 jit_solution(1098184511905874347)
XLA Ops:
  0.6 157.6 %rankmixer.1 = (bf16[256,1024]{1,0:T(8,128)(2,1)S(1)}, bf16[256,1024]{1,0:T(8,128)(2,1)S(1)}, f32[1024,512]{1,0:T(8,128)S(1)}, f32[512,1024]{1,0:T(8,128)S(1)}) custom-call(bf16[256,1024]{1,0:T(8,128)(2,1)} %bitcast.14, bf16[1024,512]{1,0:T(8,128)(2,1)} %bitcast.12, bf16[512,1024]{1,0:T(8,128)(2,1)} %bitcast.13, bf16[256,1024]{1,0:T(8,128)(2,1)} %bitcast.15), custom_call_target="tpu_custom_call" | custom-call | tf_op jit(solution)/shard_map/rankmixer/pallas_call | solution.py:456
  158.3 0.8 copy.12
  159.1 0.8 copy.13
  159.8 1.3 copy.14
  161.2 1.3 copy.15

commit v6 on v5

--- a/solution.py
+++ b/solution.py
@@ -285,11 +285,11 @@
             r = rows(i, MXU_ROWS)
             gup_ref[r, :] += dot_nt(shared_far[r, pl.ds(WIDE, WIDE)], ghid_far[:, pl.ds(WIDE, WIDE)])
 
-    for c in range(CHUNKS):
-        mix_start(tok_t, mixed, MIX, c)
     w_up().start()
     for q in range(BLOCKS):
         w_down(q).start()
+    for c in range(CHUNKS):
+        mix_start(tok_t, mixed, MIX, c)
     transpose_up(up_ref, 0)
     for q in range(BLOCKS):
         transpose_down(down_ref, 0, q)
@@ -390,12 +390,11 @@
     scatter_own(part_b, near_b, SCATTER_OWN_BACK, 1).start()
     grad_down(1, gdown_out)
     g_down().start()
-    pass_b(1, 0)
+    each_block(lambda q: pass_b(1, q))
     each_block(lambda q: scatter_z(passed_b, far_b, SCATTER_BACK, 0, q).wait_recv())
     scatter_own(part_b, near_b, SCATTER_OWN_BACK, 0).wait_recv()
     sum_back(0)
     mix_start(gsum16, mixed_back, MIX_BACK, 0)
-    pl.loop(1, BLOCKS)(lambda q: pass_b(1, q))
     grad_down(0, gdown_ref)
     each_block(lambda q: scatter_z(passed_b, far_b, SCATTER_BACK, 1, q).wait_recv())
     scatter_own(part_b, near_b, SCATTER_OWN_BACK, 1).wait_recv()
@@ -407,11 +406,11 @@
     grad_up()
     hidden_on(1).wait_recv()
     grad_up_end()
-    g_down().wait_recv()
-    gdown_ref[...] += gdown_in[...].astype(F32)
     for c in range(CHUNKS):
         mix_wait(gsum16, mixed_back, MIX_BACK, c)
         tokens_back(c)
+    g_down().wait_recv()
+    gdown_ref[...] += gdown_in[...].astype(F32)
     for copy in [w_up(), g_down(), shared_on(0), shared_on(1), hidden_on(0), hidden_on(1)]:
         copy.wait_send()
     each_block(lambda q: w_down(q).wait_send())

time: 163 us -> 161 us (0.988); the launches traced: 162 us -> 159 us
  Pallas kernels: 158 us -> 154 us
    pallas_call x1, Pallas kernels: 158 us -> 154 us  [on_device(): pl.pallas_call(functools.partial(kernel, n_token, head), out_shape=(pltpu...]
where the time goes in v6:
time: 161 us; the launch traced here: 159 us
  Pallas kernels  154 us (96%)
  local copies, waits for them, and re-layouts  4.23 us (3%)
    pallas_call x1, Pallas kernels, on_device(): pl.pallas_call(functools.partial(kernel, n_token, head), out_shape=(pltpu...  154 us
    unnamed x4, local copies, waits for them, and re-layouts  4.23 us

profile of v6, /device:TPU:1, one launch (start us, length us, event | category | flops | bytes accessed | tf_op | source)
XLA Modules:
  0.0 158.8 jit_solution(12193221817031874340)
XLA Ops:
  0.6 153.9 %rankmixer.1 = (bf16[256,1024]{1,0:T(8,128)(2,1)S(1)}, bf16[256,1024]{1,0:T(8,128)(2,1)S(1)}, f32[1024,512]{1,0:T(8,128)S(1)}, f32[512,1024]{1,0:T(8,128)S(1)}) custom-call(bf16[256,1024]{1,0:T(8,128)(2,1)} %bitcast.14, bf16[1024,512]{1,0:T(8,128)(2,1)} %bitcast.12, bf16[512,1024]{1,0:T(8,128)(2,1)} %bitcast.13, bf16[256,1024]{1,0:T(8,128)(2,1)} %bitcast.15), custom_call_target="tpu_custom_call" | custom-call | tf_op jit(solution)/shard_map/rankmixer/pallas_call | solution.py:455
  154.5 0.8 copy.12
  155.3 0.8 copy.13
  156.1 1.3 copy.14
  157.5 1.3 copy.15
